TPU v7x, 32 devices: a whole 2x2x4 slice. The times are simulated.
32 devices in a mesh: seq: 8 (over y, x, core), head: 4 (over z).
Axes of the slice: x: 2, y: 2, z: 4, core: 2. Of those that a mesh axis runs over, the one named last changes fastest.
Arguments:
- queries: bfloat16 [16384, 512], P('seq', 'head'), may hold values from -4 to 4
- key_rows: bfloat16 [16384, 512], P('seq', 'head'), may hold values from -4 to 4
- value_rows: bfloat16 [16384, 512], P('seq', 'head'), may hold values from -6 to 6
- norm_gain: float32 [512], P('head'), may hold values from 0.1 to 1.9
- out_grad: bfloat16 [16384, 512], P('seq', 'head'), may hold values from -6 to 6
Outputs:
- normed: bfloat16 [16384, 512], P('seq', 'head')
- query_grad: bfloat16 [16384, 512], P('seq', 'head')
- key_grad: bfloat16 [16384, 512], P('seq', 'head')
- value_grad: bfloat16 [16384, 512], P('seq', 'head')
All inputs are finite; a program needn't handle non-finite values.
Results may differ from a plain program's by a relative error of at most 0.0059.
Values sent between devices are 32-bit elements; how exact they have to be, the bound alone decides.
A program may use at most 64 MiB of HBM per device.

v0:
```python
import jax
import jax.numpy as jnp
from jax import lax
from jax.sharding import PartitionSpec as P

HEAD_DIM = 128
BLOCK = 512


def causal_mask(size):
    row_index = lax.broadcasted_iota(jnp.int32, (size, size), 0)
    col_index = lax.broadcasted_iota(jnp.int32, (size, size), 1)
    return row_index >= col_index


def body(queries, key_rows, value_rows, norm_gain, out_grad):
    tokens_here = queries.shape[0]
    heads_here = queries.shape[1] // HEAD_DIM
    blocks = tokens_here // BLOCK
    block_shape = (blocks, BLOCK, heads_here, HEAD_DIM)
    query4 = queries.reshape(block_shape)
    key4 = key_rows.reshape(block_shape)
    value4 = value_rows.reshape(block_shape)
    width_all = heads_here * HEAD_DIM * lax.axis_size("head")
    mask4 = causal_mask(BLOCK)[None, None]
    position = lax.axis_index("seq")
    states = jnp.einsum("bshd,bshe->bhde", key4, value4, preferred_element_type=jnp.float32)
    totals = jnp.sum(states, 0)
    piece = lax.all_gather(totals[None], "seq", axis=0, tiled=True)
    anchor = jnp.arange(piece.shape[0], dtype=jnp.int32)
    keep = (anchor < position)[:, None, None, None]
    earlier = jnp.sum(jnp.where(keep, piece, 0.0), 0)
    running = jnp.cumsum(states, 0)
    within = jnp.concatenate([jnp.zeros_like(states[:1]), running[:-1]], 0)
    prefix16 = (earlier[None] + within).astype(jnp.bfloat16)
    scores = jnp.einsum("bthd,bshd->bhts", query4, key4, preferred_element_type=jnp.float32)
    attn = jnp.where(mask4, scores, 0.0).astype(jnp.bfloat16)
    output = jnp.einsum("bhts,bshe->bthe", attn, value4, preferred_element_type=jnp.float32)
    output = output + jnp.einsum(
        "bthd,bhde->bthe", query4, prefix16, preferred_element_type=jnp.float32
    )
    gain4 = norm_gain.reshape(heads_here, HEAD_DIM)
    scaled = out_grad.reshape(block_shape).astype(jnp.float32) * gain4
    squares, products = lax.psum(
        (jnp.sum(output * output, (2, 3)), jnp.sum(scaled * output, (2, 3))), "head"
    )
    rstd = lax.rsqrt(squares / width_all + 1e-05)[:, :, None, None]
    normed = (output * rstd * gain4).astype(jnp.bfloat16).reshape(tokens_here, -1)
    mean_prod = (products / width_all)[:, :, None, None]
    dout = (rstd * scaled - output * rstd**3 * mean_prod).astype(jnp.bfloat16)
    grad_states = jnp.einsum("bthd,bthe->bhde", query4, dout, preferred_element_type=jnp.float32)
    grad_total = jnp.sum(grad_states, 0)
    piece = lax.all_gather(grad_total[None], "seq", axis=0, tiled=True)
    anchor = jnp.arange(piece.shape[0], dtype=jnp.int32)
    keep = (anchor > position)[:, None, None, None]
    later = jnp.sum(jnp.where(keep, piece, 0.0), 0)
    behind = jnp.cumsum(grad_states[::-1], 0)[::-1]
    after = jnp.concatenate([behind[1:], jnp.zeros_like(grad_states[:1])], 0)
    suffix16 = (later[None] + after).astype(jnp.bfloat16)
    bmat = jnp.einsum("bthe,bshe->bhts", dout, value4, preferred_element_type=jnp.float32)
    bmat = jnp.where(mask4, bmat, 0.0).astype(jnp.bfloat16)
    query_grad = jnp.einsum("bhts,bshd->bthd", bmat, key4, preferred_element_type=jnp.float32)
    query_grad = query_grad + jnp.einsum(
        "bthe,bhde->bthd", dout, prefix16, preferred_element_type=jnp.float32
    )
    key_grad = jnp.einsum("bhts,bthd->bshd", bmat, query4, preferred_element_type=jnp.float32)
    key_grad = key_grad + jnp.einsum(
        "bshe,bhde->bshd", value4, suffix16, preferred_element_type=jnp.float32
    )
    value_grad = jnp.einsum("bhts,bthe->bshe", attn, dout, preferred_element_type=jnp.float32)
    value_grad = value_grad + jnp.einsum(
        "bshd,bhde->bshe", key4, suffix16, preferred_element_type=jnp.float32
    )
    return (
        normed,
        query_grad.astype(jnp.bfloat16).reshape(tokens_here, -1),
        key_grad.astype(jnp.bfloat16).reshape(tokens_here, -1),
        value_grad.astype(jnp.bfloat16).reshape(tokens_here, -1),
    )


def solution(mesh):
    return jax.shard_map(
        body,
        mesh=mesh,
        in_specs=(
            P("seq", "head"),
            P("seq", "head"),
            P("seq", "head"),
            P("head"),
            P("seq", "head"),
        ),
        out_specs=(P("seq", "head"), P("seq", "head"), P("seq", "head"), P("seq", "head")),
        check_vma=False,
    )
```

profile of v0, /device:TPU:0, one launch (start us, length us, event | category | flops | bytes accessed | tf_op | source)
XLA Modules:
  0.0 71.4 jit_solution(403312878023820120)
XLA Ops:
  0.6 0.0 copy-start
  0.6 0.0 copy-start.1
  0.7 1.0 %copy-done = bf16[2048,128]{1,0:T(8,128)(2,1)S(1)} copy-done((bf16[2048,128]{1,0:T(8,128)(2,1)S(1)}, bf16[2048,128]{1,0:T(8,128)(2,1)}, u32[]{:S(2)}) %copy-start) | copy-done | bytes 524312
  1.7 0.1 iota_compare_fusion
  1.8 0.0 copy-start.9
  1.8 1.9 %select_convert_fusion.1 = bf16[4,512,512]{2,1,0:T(8,128)(2,1)S(1)} fusion(bf16[4,512,128]{2,1,0:T(8,128)(2,1)S(1)} %bitcast.81, bf16[4,512,128]{2,1,0:T(8,128)(2,1)} %bitcast.89, pred[512,512]{1,0:T(8,128)(4,1)S(1)} %iota_compare_fusion), kind=kOutput, calls=%fused_computation.1 | convolution fusion | flops 270532608 | bytes 3407872 | tf_op jit(solution)/shard_map/bthd,bshd->bhts/dot_general | solution.py:36
  3.7 0.0 copy-start.3
  3.7 0.0 copy-done.1
  3.7 1.7 %convolution_bitcast_fusion.2 = f32[4,128,512]{1,2,0:T(8,128)} fusion(bf16[4,512,512]{2,1,0:T(8,128)(2,1)S(1)} %select_convert_fusion.1, bf16[4,512,128]{2,1,0:T(8,128)(2,1)S(1)} %bitcast.85), kind=kOutput, calls=%fused_computation.4 | convolution fusion | flops 268435456 | bytes 3670016 | tf_op jit(solution)/shard_map/bhts,bshe->bthe/dot_general | solution.py:38
  5.4 0.0 copy-done.9
  5.4 0.0 copy-done.3
  5.4 0.0 copy-start.10
  5.4 0.3 fusion.26
  5.7 12.4 %all-gather = f32[1024,128]{1,0:T(8,128)} all-gather(f32[128,128]{1,0:T(8,128)S(1)} %get-tuple-element.12), channel_id=2, replica_groups=mesh['seq'=8,'head'=4] {'seq'}, dimensions={0}, use_global_device_ids=true | all-gather | bytes 589824 | tf_op jit(solution)/shard_map/all_gather | solution.py:29
  18.1 1.3 %copy.39 = f32[8,1,128,128]{2,0,3,1:T(8,128)S(1)} copy(f32[8,1,128,128]{3,2,0,1:T(8,128)} %bitcast.93) | data formatting | bytes 1048576 | tf_op jit(solution)/shard_map/all_gather | solution.py:29
  19.4 0.2 select_reduce_fusion
  19.6 0.1 copy.40
  19.7 0.0 copy-start.6
  19.7 0.2 fusion.14
  19.9 0.0 copy-done.10
  19.9 2.8 %fusion.9 = (f32[4,512]{1,0:T(4,128)S(1)}, f32[4,512]{1,0:T(4,128)S(1)}, f32[4,512,1,128]{3,1,0,2:T(8,128)}) fusion(bf16[4,512,1,128]{3,1,0,2:T(8,128)(2,1)} %bitcast.95, f32[128]{0:T(128)S(1)} %copy-done.10, f32[4,128,512]{1,2,0:T(8,128)} %convolution_bitcast_fusion.2, bf16[4,512,128]{2,1,0:T(8,128)(2,1)S(1)} %bitcast.82, ...), kind=kOutput, calls=%fused_computation.20 | convolution fusion | flops 69070848 | bytes 3424768 | tf_op jit(solution)/shard_map/bthd,bhde->bthe/dot_general | solution.py:39
  22.7 0.0 copy-done.6
  22.7 19.0 %all-reduce.2 = (f32[4,512]{1,0:T(4,128)S(1)}, f32[4,512]{1,0:T(4,128)S(1)}) all-reduce(f32[4,512]{1,0:T(4,128)S(1)} %get-tuple-element.5, f32[4,512]{1,0:T(4,128)S(1)} %get-tuple-element.4), channel_id=1, replica_groups=mesh['seq'=8,'head'=4] {'head'}, use_global_device_ids=true, to_apply=%region_4.5 | all-reduce | flops 4096 | bytes 32768 | tf_op jit(solution)/shard_map/psum | solution.py:44
  41.7 2.8 %fusion.10 = (bf16[4,512,128]{2,1,0:T(8,128)(2,1)S(1)}, bf16[4,512,1,128]{3,1,0,2:T(8,128)(2,1)}) fusion(f32[4,512,1,128]{3,1,0,2:T(8,128)} %get-tuple-element.14, f32[4,512]{1,0:T(4,128)S(1)} %get-tuple-element.17, f32[4,512]{1,0:T(4,128)S(1)} %get-tuple-element.10, f32[128]{0:T(128)S(1)} %copy-done.10, f32[4,512]{1,0:T(4,128)S(1)} %get-tuple-element.11, ...), kind=kLoop, calls=%fused_computation.24 | loop fusion | flops 2621440 | bytes 2646528 | tf_op jit(solution)/shard_map/reshape.36
  44.5 1.5 %fusion.28 = f32[4,128,512]{2,1,0:T(8,128)} fusion(bf16[4,512,128]{2,1,0:T(8,128)(2,1)S(1)} %get-tuple-element.8, bf16[4,512,512]{2,1,0:T(8,128)(2,1)S(1)} %select_convert_fusion.1), kind=kOutput, calls=%fused_computation.47 | convolution fusion | flops 268435456 | bytes 3670016 | tf_op jit(solution)/shard_map/bhts,bthe->bshe/dot_general | solution.py:70
  46.0 1.0 %fusion.27 = (f32[128,128]{0,1:T(8,128)S(1)}, f32[4,128,128]{1,2,0:T(8,128)}) fusion(bf16[4,512,128]{2,1,0:T(8,128)(2,1)S(1)} %get-tuple-element.8, bf16[4,512,128]{2,1,0:T(8,128)(2,1)S(1)} %bitcast.84), kind=kOutput, calls=%fused_computation.46 | convolution fusion | flops 67158016 | bytes 1376256 | tf_op jit(solution)/shard_map/bthd,bthe->bhde/dot_general | solution.py:51
  47.1 0.0 copy-start.5
  47.1 11.0 %all-gather.1 = f32[1024,128]{0,1:T(8,128)S(1)} all-gather(f32[128,128]{0,1:T(8,128)S(1)} %get-tuple-element.15), channel_id=3, replica_groups=mesh['seq'=8,'head'=4] {'seq'}, dimensions={0}, use_global_device_ids=true | all-gather | bytes 589824 | tf_op jit(solution)/shard_map/all_gather | solution.py:53
  58.0 0.1 copy.59
  58.1 0.8 %fusion.11 = f32[128,128]{0,1:T(8,128)} fusion(f32[16,8,8,128]{3,2,1,0:T(8,128)S(1)} %copy.59, pred[8]{0:T(512)(128)(4,1)S(1)} %iota_compare_fusion.1), kind=kLoop, calls=%fused_computation.26 | loop fusion | flops 245760 | bytes 589832 | tf_op jit(solution)/shard_map/reduce_sum | solution.py:56
  59.0 1.0 %reverse.4 = f32[4,128,128]{1,2,0:T(8,128)S(1)} reverse(f32[4,128,128]{1,2,0:T(8,128)} %get-tuple-element.16), dimensions={0} | reverse | bytes 524288 | tf_op jit(solution)/shard_map/reverse
  59.9 0.2 fusion.12
  60.1 0.0 copy-start.2
  60.1 0.7 slice.13
  60.8 0.9 %slice.11 = f32[3,1,128,128]{2,3,0,1:T(8,128)S(1)} reverse(f32[3,1,128,128]{2,3,0,1:T(8,128)} %slice.13), dimensions={0} | reverse | bytes 393216 | tf_op jit(solution)/shard_map/slice | solution.py:58
  61.8 0.0 copy-done.4
  61.8 0.0 copy-done.5
  61.8 1.9 %fusion.4 = bf16[4,512,1,128]{1,3,0,2:T(8,128)(2,1)} fusion(f32[4,128,512]{2,1,0:T(8,128)S(1)} %copy-done.5, bf16[4,512,128]{2,1,0:T(8,128)(2,1)S(1)} %bitcast.91, f32[3,1,128,128]{2,3,0,1:T(8,128)S(1)} %slice.11, f32[128,128]{0,1:T(8,128)} %fusion.11), kind=kOutput, calls=%fused_computation.13 | convolution fusion | flops 67764224 | bytes 2359296 | tf_op jit(solution)/shard_map/bshd,bhde->bshe/dot_general | solution.py:71
  63.7 2.0 %copy.49 = bf16[4,512,1,128]{3,1,0,2:T(8,128)(2,1)} copy(bf16[4,512,1,128]{1,3,0,2:T(8,128)(2,1)} %fusion.4) | data formatting | bytes 1048576 | tf_op jit(solution)/shard_map/convert_element_type | solution.py:78
  65.8 0.0 copy-done.2
  65.8 1.7 %select_convert_fusion = bf16[4,512,512]{2,1,0:T(8,128)(2,1)S(1)} fusion(bf16[4,512,128]{2,1,0:T(8,128)(2,1)S(1)} %get-tuple-element.8, bf16[4,512,128]{2,1,0:T(8,128)(2,1)S(1)} %bitcast.87, pred[512,512]{1,0:T(8,128)(4,1)} %copy-done.9), kind=kOutput, calls=%fused_computation | convolution fusion | flops 270532608 | bytes 3407872 | tf_op jit(solution)/shard_map/bthe,bshe->bhts/dot_general | solution.py:60
  67.5 0.0 copy-start.8
  67.5 0.9 %convolution_bitcast_fusion = f32[4,128,512]{1,2,0:T(8,128)S(1)} fusion(bf16[4,512,512]{2,1,0:T(8,128)(2,1)S(1)} %select_convert_fusion, bf16[4,512,128]{2,1,0:T(8,128)(2,1)S(1)} %bitcast.83), kind=kOutput, calls=%fused_computation.2 | convolution fusion | flops 268435456 | bytes 3670016 | tf_op jit(solution)/shard_map/bhts,bthd->bshd/dot_general | solution.py:66
  68.4 0.0 copy-done.8
  68.4 1.1 %fusion.3 = bf16[4,128,512]{1,2,0:T(8,128)(2,1)} fusion(f32[4,128,512]{1,2,0:T(8,128)S(1)} %convolution_bitcast_fusion, bf16[4,512,128]{2,1,0:T(8,128)(2,1)S(1)} %bitcast.88, f32[3,1,128,128]{2,3,0,1:T(8,128)S(1)} %slice.11, f32[128,128]{0,1:T(8,128)S(1)} %copy-done.8), kind=kOutput, calls=%fused_computation.12 | convolution fusion | flops 67764224 | bytes 2359296 | tf_op jit(solution)/shard_map/bshe,bhde->bshd/dot_general | solution.py:67
  69.5 0.7 convolution_bitcast_fusion.1
  70.2 0.1 copy-done.7
  70.3 1.1 %fusion.1 = bf16[4,128,512]{1,2,0:T(8,128)(2,1)} fusion(f32[4,128,512]{1,2,0:T(8,128)S(1)} %convolution_bitcast_fusion.1, bf16[4,512,128]{2,1,0:T(8,128)(2,1)S(1)} %get-tuple-element.8, f32[3,1,128,128]{3,2,0,1:T(8,128)S(1)} %slice.12, f32[128,128]{1,0:T(8,128)S(1)} %copy-done.7), kind=kOutput, calls=%fused_computation.10 | convolution fusion | flops 67764224 | bytes 2359296 | tf_op jit(solution)/shard_map/bthe,bhde->bthd/dot_general | solution.py:63
  (6 shorter events, 0.0 us)
Async XLA Ops:
  0.6 1.0 %copy-start = (bf16[2048,128]{1,0:T(8,128)(2,1)S(1)}, bf16[2048,128]{1,0:T(8,128)(2,1)}, u32[]{:S(2)}) copy-start(bf16[2048,128]{1,0:T(8,128)(2,1)} %param.5) | copy-start | bytes 1572868
  0.6 3.0 %copy-start.1 = (bf16[2048,128]{1,0:T(8,128)(2,1)S(1)}, bf16[2048,128]{1,0:T(8,128)(2,1)}, u32[]{:S(2)}) copy-start(bf16[2048,128]{1,0:T(8,128)(2,1)} %param.7) | copy-start | bytes 1572868
  1.8 3.6 %copy-start.9 = (pred[512,512]{1,0:T(8,128)(4,1)}, pred[512,512]{1,0:T(8,128)(4,1)S(1)}, u32[]{:S(2)}) copy-start(pred[512,512]{1,0:T(8,128)(4,1)S(1)} %iota_compare_fusion) | copy-start | bytes 786436
  3.7 1.7 %copy-start.3 = (bf16[2048,128]{1,0:T(8,128)(2,1)S(1)}, bf16[2048,128]{1,0:T(8,128)(2,1)}, u32[]{:S(2)}) copy-start(bf16[2048,128]{1,0:T(8,128)(2,1)} %param.6) | copy-start | bytes 1572868
  5.4 14.5 %copy-start.10 = (f32[128]{0:T(128)S(1)}, f32[128]{0:T(128)}, u32[]{:S(2)}) copy-start(f32[128]{0:T(128)} %param.8) | copy-start | bytes 1540
  19.7 3.0 %copy-start.6 = (f32[128,128]{1,0:T(8,128)}, f32[128,128]{1,0:T(8,128)S(1)}, u32[]{:S(2)}) copy-start(f32[128,128]{1,0:T(8,128)S(1)} %copy.40) | copy-start | bytes 196612
  47.1 14.7 %copy-start.4 = (bf16[2048,128]{1,0:T(8,128)(2,1)S(1)}, bf16[2048,128]{1,0:T(8,128)(2,1)}, u32[]{:S(2)}) copy-start(bf16[2048,128]{1,0:T(8,128)(2,1)} %param.6) | copy-start | bytes 1572868
  47.1 14.7 %copy-start.5 = (f32[4,128,512]{2,1,0:T(8,128)S(1)}, f32[4,128,512]{2,1,0:T(8,128)}, u32[]{:S(2)}) copy-start(f32[4,128,512]{2,1,0:T(8,128)} %fusion.28) | copy-start | bytes 3145732
  60.1 5.6 %copy-start.2 = (bf16[2048,128]{1,0:T(8,128)(2,1)S(1)}, bf16[2048,128]{1,0:T(8,128)(2,1)}, u32[]{:S(2)}) copy-start(bf16[2048,128]{1,0:T(8,128)(2,1)} %param.7) | copy-start | bytes 1572868
  67.5 0.9 %copy-start.8 = (f32[128,128]{0,1:T(8,128)S(1)}, f32[128,128]{0,1:T(8,128)}, u32[]{:S(2)}) copy-start(f32[128,128]{0,1:T(8,128)} %fusion.11) | copy-start | bytes 196612
  69.5 0.8 %copy-start.7 = (f32[128,128]{1,0:T(8,128)S(1)}, f32[128,128]{1,0:T(8,128)}, u32[]{:S(2)}) copy-start(f32[128,128]{1,0:T(8,128)} %copy-done.6) | copy-start | bytes 196612
where the time goes:
time: 72 us; the launch traced here: 71.4 us
  blocking collectives  42.3 us (59%)
  matrix products  16.7 us (23%)
  local copies, waits for them, and re-layouts  7.31 us (10%)
  other arithmetic  4.29 us (6%)
  between operations  0.84 us (1%)
    psum x1, blocking collectives, body(): lax.psum((jnp.sum(output * output, (2, 3)), jnp.sum(scaled * output, (2,...  19 us
    all_gather x1, blocking collectives, body(): piece = lax.all_gather(totals[None], 'seq', axis=0, tiled=True)  12.4 us
    all_gather x1, blocking collectives, body(): piece = lax.all_gather(grad_total[None], 'seq', axis=0, tiled=True)  11 us
    another operation x1, other arithmetic  2.8 us
    dot_general x1, matrix products, body(): jnp.einsum('bthd,bhde->bthe', query4, prefix16, preferred_element_type=jn...  2.79 us
    convert_element_type x1, local copies, waits for them, and re-layouts, body(): value_grad.astype(jnp.bfloat16).reshape(tokens_here, -1)  2.04 us
    dot_general x1, matrix products, body(): jnp.einsum('bshd,bhde->bshe', key4, suffix16, preferred_element_type=jnp....  1.94 us
    dot_general x1, matrix products, body(): jnp.einsum('bthd,bshd->bhts', query4, key4, preferred_element_type=jnp.fl...  1.88 us

commit v1 on v0

--- a/solution.py
+++ b/solution.py
@@ -14,6 +14,29 @@
 
 
 def body(queries, key_rows, value_rows, norm_gain, out_grad):
+
+    def _review_group(tile_in, across):
+        reached = lax.axis_size(across)
+        current_value = lax.axis_index(across)
+        val2, last, field_out = (reached, current_value, tile_in.shape[0])
+        slots = [(m, (m + 1) % val2) for m in range(val2)]
+        line_up = [(m, (m - 1) % val2) for m in range(val2)]
+        e_now = jnp.zeros((*tile_in.shape[:0], val2 * field_out, *tile_in.shape[1:]), tile_in.dtype)
+        e_now = lax.dynamic_update_slice_in_dim(e_now, tile_in, last * field_out, axis=0)
+        local_part = local_now = tile_in
+        s_next = val2 // 2
+        for i in range(1, s_next + 1):
+            local_part = lax.ppermute(local_part, across, slots)
+            e_now = lax.dynamic_update_slice_in_dim(
+                e_now, local_part, (last - i) % val2 * field_out, axis=0
+            )
+            if i < val2 - s_next:
+                local_now = lax.ppermute(local_now, across, line_up)
+                e_now = lax.dynamic_update_slice_in_dim(
+                    e_now, local_now, (last + i) % val2 * field_out, axis=0
+                )
+        return e_now
+
     tokens_here = queries.shape[0]
     heads_here = queries.shape[1] // HEAD_DIM
     blocks = tokens_here // BLOCK
@@ -26,7 +49,7 @@
     position = lax.axis_index("seq")
     states = jnp.einsum("bshd,bshe->bhde", key4, value4, preferred_element_type=jnp.float32)
     totals = jnp.sum(states, 0)
-    piece = lax.all_gather(totals[None], "seq", axis=0, tiled=True)
+    piece = _review_group(totals[None], "seq")
     anchor = jnp.arange(piece.shape[0], dtype=jnp.int32)
     keep = (anchor < position)[:, None, None, None]
     earlier = jnp.sum(jnp.where(keep, piece, 0.0), 0)

time: 72 us -> 89.2 us (1.24)
  local copies, waits for them, and re-layouts: 7.31 us -> 21.2 us
  blocking collectives: 42.3 us -> 30.6 us
  starting transfers between devices: 0 us -> 9.04 us
  matrix products: 16.7 us -> 19.7 us
  waiting for transfers between devices: 0 us -> 2.19 us
    all_gather x1 -> x0, blocking collectives: 12.4 us -> none  [body(): piece = lax.all_gather(totals[None], 'seq', axis=0, tiled=True)]
    dynamic_update_slice x0 -> x8, local copies, waits for them, and re-layouts: none -> 11.5 us  [the longest x4 5.74 us: _review_group(): lax.dynamic_update_slice_in_dim(e_now, local_part, (last - i) % val2 * fi...]
    ppermute x0 -> x7, starting transfers between devices: none -> 9.04 us  [the longest x3 8.52 us: _review_group(): local_now = lax.ppermute(local_now, across, line_up)]
    ppermute x0 -> x7, local copies, waits for them, and re-layouts: none -> 4.81 us  [the longest x4 2.87 us: _review_group(): local_part = lax.ppermute(local_part, across, slots)]
    ppermute x0 -> x7, waiting for transfers between devices: none -> 2.19 us  [the longest x3 1.92 us: _review_group(): local_now = lax.ppermute(local_now, across, line_up)]
    slice x2, local copies, waits for them, and re-layouts: 1.63 us -> 0.03 us  [body(): after = jnp.concatenate([behind[1:], jnp.zeros_like(grad_states[:1])], 0)]
    all_gather x1 -> x0, local copies, waits for them, and re-layouts: 1.27 us -> none  [body(): piece = lax.all_gather(totals[None], 'seq', axis=0, tiled=True)]
    dot_general x1, matrix products: 1.09 us -> 2.35 us  [body(): jnp.einsum('bshe,bhde->bshd', value4, suffix16, preferred_element_type=jn...]
  transfers between devices with their start and end apart: 0 -> 7, of which waited for: 0 -> 2; matrix products, arithmetic and copies ran while one was open for 0% -> 20% of each run, Pallas kernels for 0% -> 0%
where the time goes in v1:
time: 89.2 us; the launch traced here: 88.6 us
  blocking collectives  30.6 us (34%)
  local copies, waits for them, and re-layouts  21.2 us (24%)
  matrix products  19.7 us (22%)
  starting transfers between devices  9.04 us (10%)
  other arithmetic  4.77 us (5%)
  waiting for transfers between devices  2.19 us (2%)
  between operations  1.16 us (1%)
    psum x1, blocking collectives, body(): lax.psum((jnp.sum(output * output, (2, 3)), jnp.sum(scaled * output, (2,...  19.7 us
    all_gather x1, blocking collectives, body(): piece = lax.all_gather(grad_total[None], 'seq', axis=0, tiled=True)  10.9 us
    ppermute x3, starting transfers between devices, _review_group(): local_now = lax.ppermute(local_now, across, line_up)  8.52 us
    dynamic_update_slice x4, local copies, waits for them, and re-layouts, _review_group(): lax.dynamic_update_slice_in_dim(e_now, local_part, (last - i) % val2 * fi...  5.74 us
    dynamic_update_slice x3, local copies, waits for them, and re-layouts, _review_group(): lax.dynamic_update_slice_in_dim(e_now, local_now, (last + i) % val2 * fie...  4.31 us
    ppermute x4, local copies, waits for them, and re-layouts, _review_group(): local_part = lax.ppermute(local_part, across, slots)  2.87 us
    another operation x1, other arithmetic  2.8 us
    dot_general x1, matrix products, body(): jnp.einsum('bthd,bhde->bthe', query4, prefix16, preferred_element_type=jn...  2.8 us
  transfers between devices with their start and end apart: 7, of which 2 were waited for; matrix products, arithmetic and copies ran while one was open for 20% of the time, Pallas kernels for 0%

profile of v1, /device:TPU:0, one launch (start us, length us, event | category | flops | bytes accessed | tf_op | source)
XLA Modules:
  0.0 88.6 jit_solution(16194354359336651389)
XLA Ops:
  0.6 0.0 copy-start
  0.6 1.6 %fusion.26 = (f32[128,128]{1,0:T(8,128)S(1)}, f32[4,128,128]{2,1,0:T(8,128)S(1)}) fusion(bf16[4,512,128]{2,1,0:T(8,128)(2,1)} %bitcast.85, bf16[4,512,128]{2,1,0:T(8,128)(2,1)} %bitcast.89), kind=kOutput, calls=%fused_computation.45 | convolution fusion | flops 67158016 | bytes 1376256 | tf_op jit(solution)/shard_map/bshd,bshe->bhde/dot_general | solution.py:50
  2.3 0.5 collective-permute-start
  2.8 2.9 %collective-permute-start.1 = (f32[1,1,128,128]{3,2,1,0:T(8,128)S(1)}, f32[1,1,128,128]{3,2,1,0:T(8,128)S(1)}, u32[]{:S(2)}, u32[]{:S(2)}) collective-permute-start(f32[1,1,128,128]{3,2,1,0:T(8,128)S(1)} %bitcast.100), channel_id=1, source_target_pairs={{0,28},{4,0},{8,4},{12,8},{16,12},{20,16},{24,20},{28,24},{1,29},{... | collective-permute-start | bytes 196616 | tf_op jit(solution)/shard_map/ppermute | solution.py:34
  5.7 0.1 iota_compare_fusion
  5.8 1.9 %select_convert_fusion.1 = bf16[4,512,512]{2,1,0:T(8,128)(2,1)S(1)} fusion(bf16[4,512,128]{2,1,0:T(8,128)(2,1)S(1)} %bitcast.81, bf16[4,512,128]{2,1,0:T(8,128)(2,1)} %bitcast.86, pred[512,512]{1,0:T(8,128)(4,1)S(1)} %iota_compare_fusion), kind=kOutput, calls=%fused_computation.1 | convolution fusion | flops 270532608 | bytes 3407872 | tf_op jit(solution)/shard_map/bthd,bshd->bhts/dot_general | solution.py:59
  7.7 1.7 %convolution_bitcast_fusion.2 = f32[4,128,512]{1,2,0:T(8,128)} fusion(bf16[4,512,512]{2,1,0:T(8,128)(2,1)S(1)} %select_convert_fusion.1, bf16[4,512,128]{2,1,0:T(8,128)(2,1)S(1)} %bitcast.90), kind=kOutput, calls=%fused_computation.4 | convolution fusion | flops 268435456 | bytes 3670016 | tf_op jit(solution)/shard_map/bhts,bshe->bthe/dot_general | solution.py:61
  9.4 0.2 fusion.14
  9.6 0.1 copy.39
  9.9 1.4 %dynamic_update_slice.24 = f32[8,1,128,128]{2,0,3,1:T(8,128)S(1)} dynamic-update-slice(f32[8,1,128,128]{2,0,3,1:T(8,128)S(1)} %broadcast_in_dim.53, f32[1,1,128,128]{2,0,3,1:T(1,128)S(1)} %copy.39, s32[]{:T(128)S(6)} %select_n.72, s32[]{:T(128)} %constant.61.clone.1, s32[]{:T(128)} %constant.61.clone.1, s32[]{:T(128)} %constant.61.clone.1) | dynamic-update-slice | bytes 131076 | tf_op jit(solution)/shard_map/dynamic_update_slice | solution.py:25
  11.4 2.7 %collective-permute-start.3 = (f32[1,1,128,128]{3,2,1,0:T(8,128)S(1)}, f32[1,1,128,128]{3,2,1,0:T(8,128)}, u32[]{:S(2)}, u32[]{:S(2)}) collective-permute-start(f32[1,1,128,128]{3,2,1,0:T(8,128)S(1)} %collective-permute-done.1), channel_id=1, source_target_pairs={{0,28},{4,0},{8,4},{12,8},{16,12},{20,16},{24,20},{28,24},{1,29},{... | collective-permute-start | bytes 196616 | tf_op jit(solution)/shard_map/ppermute | solution.py:34
  14.1 0.3 collective-permute-done.2
  14.3 1.9 %collective-permute-done.3 = f32[1,1,128,128]{3,2,1,0:T(8,128)} collective-permute-done((f32[1,1,128,128]{3,2,1,0:T(8,128)S(1)}, f32[1,1,128,128]{3,2,1,0:T(8,128)}, u32[]{:S(2)}, u32[]{:S(2)}) %collective-permute-start.3) | collective-permute-done | bytes 65568 | tf_op jit(solution)/shard_map/ppermute | solution.py:34
  16.3 2.9 %collective-permute-start.5 = (f32[1,1,128,128]{3,2,1,0:T(8,128)}, f32[1,1,128,128]{3,2,1,0:T(8,128)}, u32[]{:S(2)}, u32[]{:S(2)}) collective-permute-start(f32[1,1,128,128]{3,2,1,0:T(8,128)} %collective-permute-done.3), channel_id=1, source_target_pairs={{0,28},{4,0},{8,4},{12,8},{16,12},{20,16},{24,20},{28,24},{1,29},{... | collective-permute-start | bytes 196616 | tf_op jit(solution)/shard_map/ppermute | solution.py:34
  19.2 0.9 %copy.40 = f32[1,1,128,128]{2,0,3,1:T(1,128)S(1)} copy(f32[1,1,128,128]{3,2,1,0:T(8,128)} %collective-permute-done) | data formatting | bytes 131072 | tf_op jit(solution)/shard_map/ppermute | solution.py:29
  20.1 1.4 %dynamic_update_slice.25 = f32[8,1,128,128]{2,0,3,1:T(8,128)S(1)} dynamic-update-slice(f32[8,1,128,128]{2,0,3,1:T(8,128)S(1)} %dynamic_update_slice.24, f32[1,1,128,128]{2,0,3,1:T(1,128)S(1)} %copy.40, s32[]{:T(128)S(6)} %select_n.74, s32[]{:T(128)} %constant.61.clone.1, s32[]{:T(128)} %constant.61.clone.1, s32[]{:T(128)} %constant.61.clone.1) | dynamic-update-slice | bytes 131076 | tf_op jit(solution)/shard_map/dynamic_update_slice | solution.py:30
  21.6 0.1 copy.41
  21.7 1.4 %dynamic_update_slice.26 = f32[8,1,128,128]{2,0,3,1:T(8,128)S(1)} dynamic-update-slice(f32[8,1,128,128]{2,0,3,1:T(8,128)S(1)} %dynamic_update_slice.25, f32[1,1,128,128]{2,0,3,1:T(1,128)S(1)} %copy.41, s32[]{:T(128)S(6)} %select_n.76, s32[]{:T(128)} %constant.61.clone.1, s32[]{:T(128)} %constant.61.clone.1, s32[]{:T(128)} %constant.61.clone.1) | dynamic-update-slice | bytes 131076 | tf_op jit(solution)/shard_map/dynamic_update_slice | solution.py:35
  23.1 0.9 %copy.42 = f32[1,1,128,128]{2,0,3,1:T(1,128)S(1)} copy(f32[1,1,128,128]{3,2,1,0:T(8,128)} %collective-permute-done.2) | data formatting | bytes 131072 | tf_op jit(solution)/shard_map/ppermute | solution.py:29
  24.0 1.4 %dynamic_update_slice.27 = f32[8,1,128,128]{2,0,3,1:T(8,128)S(1)} dynamic-update-slice(f32[8,1,128,128]{2,0,3,1:T(8,128)S(1)} %dynamic_update_slice.26, f32[1,1,128,128]{2,0,3,1:T(1,128)S(1)} %copy.42, s32[]{:T(128)S(6)} %select_n.78, s32[]{:T(128)} %constant.61.clone.1, s32[]{:T(128)} %constant.61.clone.1, s32[]{:T(128)} %constant.61.clone.1) | dynamic-update-slice | bytes 131076 | tf_op jit(solution)/shard_map/dynamic_update_slice | solution.py:30
  25.5 0.9 %copy.43 = f32[1,1,128,128]{2,0,3,1:T(1,128)S(1)} copy(f32[1,1,128,128]{3,2,1,0:T(8,128)} %collective-permute-done.3) | data formatting | bytes 131072 | tf_op jit(solution)/shard_map/ppermute | solution.py:34
  26.4 1.4 %dynamic_update_slice.28 = f32[8,1,128,128]{2,0,3,1:T(8,128)S(1)} dynamic-update-slice(f32[8,1,128,128]{2,0,3,1:T(8,128)S(1)} %dynamic_update_slice.27, f32[1,1,128,128]{2,0,3,1:T(1,128)S(1)} %copy.43, s32[]{:T(128)S(6)} %select_n.80, s32[]{:T(128)} %constant.61.clone.1, s32[]{:T(128)} %constant.61.clone.1, s32[]{:T(128)} %constant.61.clone.1) | dynamic-update-slice | bytes 131076 | tf_op jit(solution)/shard_map/dynamic_update_slice | solution.py:35
  27.9 0.1 copy.44
  28.0 1.4 %dynamic_update_slice.29 = f32[8,1,128,128]{2,0,3,1:T(8,128)S(1)} dynamic-update-slice(f32[8,1,128,128]{2,0,3,1:T(8,128)S(1)} %dynamic_update_slice.28, f32[1,1,128,128]{2,0,3,1:T(1,128)S(1)} %copy.44, s32[]{:T(128)S(6)} %select_n.82, s32[]{:T(128)} %constant.61.clone.1, s32[]{:T(128)} %constant.61.clone.1, s32[]{:T(128)} %constant.61.clone.1) | dynamic-update-slice | bytes 131076 | tf_op jit(solution)/shard_map/dynamic_update_slice | solution.py:30
  29.4 0.9 %copy.45 = f32[1,1,128,128]{2,0,3,1:T(1,128)S(1)} copy(f32[1,1,128,128]{3,2,1,0:T(8,128)} %collective-permute-done.5) | data formatting | bytes 131072 | tf_op jit(solution)/shard_map/ppermute | solution.py:34
  30.3 1.4 %dynamic_update_slice.30 = f32[8,1,128,128]{2,0,3,1:T(8,128)S(1)} dynamic-update-slice(f32[8,1,128,128]{2,0,3,1:T(8,128)S(1)} %dynamic_update_slice.29, f32[1,1,128,128]{2,0,3,1:T(1,128)S(1)} %copy.45, s32[]{:T(128)S(6)} %select_n.84, s32[]{:T(128)} %constant.61.clone.1, s32[]{:T(128)} %constant.61.clone.1, s32[]{:T(128)} %constant.61.clone.1) | dynamic-update-slice | bytes 131076 | tf_op jit(solution)/shard_map/dynamic_update_slice | solution.py:35
  31.8 0.9 %copy.46 = f32[1,1,128,128]{2,0,3,1:T(1,128)S(1)} copy(f32[1,1,128,128]{3,2,1,0:T(8,128)} %collective-permute-done.6) | data formatting | bytes 131072 | tf_op jit(solution)/shard_map/ppermute | solution.py:29
  32.7 1.4 %dynamic_update_slice.31 = f32[8,1,128,128]{2,0,3,1:T(8,128)S(1)} dynamic-update-slice(f32[8,1,128,128]{2,0,3,1:T(8,128)S(1)} %dynamic_update_slice.30, f32[1,1,128,128]{2,0,3,1:T(1,128)S(1)} %copy.46, s32[]{:T(128)S(6)} %select_n.86, s32[]{:T(128)} %constant.61.clone.1, s32[]{:T(128)} %constant.61.clone.1, s32[]{:T(128)} %constant.61.clone.1) | dynamic-update-slice | bytes 131076 | tf_op jit(solution)/shard_map/dynamic_update_slice | solution.py:30
  34.2 0.2 select_reduce_fusion
  34.4 0.1 copy.47
  34.5 2.8 %fusion.9 = (f32[4,512]{1,0:T(4,128)S(1)}, f32[4,512]{1,0:T(4,128)S(1)}, f32[4,512,1,128]{3,1,0,2:T(8,128)}) fusion(bf16[4,512,1,128]{3,1,0,2:T(8,128)(2,1)} %bitcast.94, f32[128]{0:T(128)S(1)} %copy-done.10, f32[4,128,512]{1,2,0:T(8,128)} %convolution_bitcast_fusion.2, bf16[4,512,128]{2,1,0:T(8,128)(2,1)S(1)} %bitcast.82, ...), kind=kOutput, calls=%fused_computation.20 | convolution fusion | flops 69070848 | bytes 3424768 | tf_op jit(solution)/shard_map/bthd,bhde->bthe/dot_general | solution.py:62
  37.3 19.7 %all-reduce.2 = (f32[4,512]{1,0:T(4,128)S(1)}, f32[4,512]{1,0:T(4,128)S(1)}) all-reduce(f32[4,512]{1,0:T(4,128)S(1)} %get-tuple-element.5, f32[4,512]{1,0:T(4,128)S(1)} %get-tuple-element.4), channel_id=1, replica_groups=mesh['seq'=8,'head'=4] {'head'}, use_global_device_ids=true, to_apply=%region_4.5 | all-reduce | flops 4096 | bytes 32768 | tf_op jit(solution)/shard_map/psum | solution.py:67
  57.0 2.8 %fusion.10 = (bf16[4,512,128]{2,1,0:T(8,128)(2,1)S(1)}, bf16[4,512,1,128]{3,1,0,2:T(8,128)(2,1)}) fusion(f32[4,512,1,128]{3,1,0,2:T(8,128)} %get-tuple-element.14, f32[4,512]{1,0:T(4,128)S(1)} %get-tuple-element.17, f32[4,512]{1,0:T(4,128)S(1)} %get-tuple-element.10, f32[128]{0:T(128)S(1)} %copy-done.10, f32[4,512]{1,0:T(4,128)S(1)} %get-tuple-element.11, ...), kind=kLoop, calls=%fused_computation.24 | loop fusion | flops 2621440 | bytes 2646528 | tf_op jit(solution)/shard_map/reshape.36
  59.8 1.5 %fusion.28 = f32[4,128,512]{2,1,0:T(8,128)} fusion(bf16[4,512,128]{2,1,0:T(8,128)(2,1)S(1)} %get-tuple-element.8, bf16[4,512,512]{2,1,0:T(8,128)(2,1)S(1)} %select_convert_fusion.1), kind=kOutput, calls=%fused_computation.47 | convolution fusion | flops 268435456 | bytes 3670016 | tf_op jit(solution)/shard_map/bhts,bthe->bshe/dot_general | solution.py:93
  61.4 1.1 %fusion.27 = (f32[128,128]{0,1:T(8,128)S(1)}, f32[4,128,128]{1,2,0:T(8,128)}) fusion(bf16[4,512,128]{2,1,0:T(8,128)(2,1)S(1)} %get-tuple-element.8, bf16[4,512,128]{2,1,0:T(8,128)(2,1)S(1)} %bitcast.84), kind=kOutput, calls=%fused_computation.46 | convolution fusion | flops 67158016 | bytes 1376256 | tf_op jit(solution)/shard_map/bthd,bthe->bhde/dot_general | solution.py:74
  62.4 0.8 select_convert_fusion
  63.2 1.9 %convolution_bitcast_fusion = f32[4,128,512]{1,2,0:T(8,128)} fusion(bf16[4,512,512]{2,1,0:T(8,128)(2,1)S(1)} %select_convert_fusion, bf16[4,512,128]{2,1,0:T(8,128)(2,1)S(1)} %bitcast.83), kind=kOutput, calls=%fused_computation.2 | convolution fusion | flops 268435456 | bytes 3670016 | tf_op jit(solution)/shard_map/bhts,bthd->bshd/dot_general | solution.py:89
  65.1 0.7 convolution_bitcast_fusion.1
  65.8 10.9 %all-gather = f32[1024,128]{0,1:T(8,128)S(1)} all-gather(f32[128,128]{0,1:T(8,128)S(1)} %get-tuple-element.15), channel_id=2, replica_groups=mesh['seq'=8,'head'=4] {'seq'}, dimensions={0}, use_global_device_ids=true | all-gather | bytes 589824 | tf_op jit(solution)/shard_map/all_gather | solution.py:76
  76.7 0.9 %copy.66 = f32[16,8,8,128]{3,2,1,0:T(8,128)} copy(f32[16,8,8,128]{3,1,2,0:T(8,128)S(1)} %bitcast.93) | data formatting | bytes 1048576
  77.6 1.0 %reverse.4 = f32[4,128,128]{1,2,0:T(8,128)S(1)} reverse(f32[4,128,128]{1,2,0:T(8,128)} %get-tuple-element.16), dimensions={0} | reverse | bytes 524288 | tf_op jit(solution)/shard_map/reverse
  78.6 0.2 fusion.12
  78.8 1.3 %fusion.11 = f32[128,128]{0,1:T(8,128)S(1)} fusion(f32[16,8,8,128]{3,2,1,0:T(8,128)} %copy.66, pred[8]{0:T(512)(128)(4,1)S(1)} %iota_compare_fusion.1), kind=kLoop, calls=%fused_computation.26 | loop fusion | flops 245760 | bytes 589832 | tf_op jit(solution)/shard_map/reduce_sum | solution.py:79
  80.1 0.6 copy-done.7
  80.8 2.3 %fusion.4 = bf16[4,512,1,128]{1,3,0,2:T(8,128)(2,1)} fusion(f32[4,128,512]{2,1,0:T(8,128)} %fusion.28, bf16[4,512,128]{2,1,0:T(8,128)(2,1)S(1)} %bitcast.88, f32[3,1,128,128]{2,3,0,1:T(8,128)S(1)} %slice.11, f32[128,128]{0,1:T(8,128)S(1)} %fusion.11), kind=kOutput, calls=%fused_computation.13 | convolution fusion | flops 67764224 | bytes 2359296 | tf_op jit(solution)/shard_map/bshd,bhde->bshe/dot_general | solution.py:94
  83.1 2.1 %copy.56 = bf16[4,512,1,128]{3,1,0,2:T(8,128)(2,1)} copy(bf16[4,512,1,128]{1,3,0,2:T(8,128)(2,1)} %fusion.4) | data formatting | bytes 1048576 | tf_op jit(solution)/shard_map/convert_element_type | solution.py:101
  85.1 2.3 %fusion.3 = bf16[4,128,512]{1,2,0:T(8,128)(2,1)} fusion(f32[4,128,512]{1,2,0:T(8,128)} %convolution_bitcast_fusion, bf16[4,512,128]{2,1,0:T(8,128)(2,1)S(1)} %bitcast.92, f32[3,1,128,128]{2,3,0,1:T(8,128)S(1)} %slice.11, f32[128,128]{0,1:T(8,128)} %copy-done.7), kind=kOutput, calls=%fused_computation.12 | convolution fusion | flops 67764224 | bytes 2359296 | tf_op jit(solution)/shard_map/bshe,bhde->bshd/dot_general | solution.py:90
  87.5 1.1 %fusion.1 = bf16[4,128,512]{1,2,0:T(8,128)(2,1)} fusion(f32[4,128,512]{1,2,0:T(8,128)S(1)} %convolution_bitcast_fusion.1, bf16[4,512,128]{2,1,0:T(8,128)(2,1)S(1)} %get-tuple-element.8, f32[3,1,128,128]{3,2,0,1:T(8,128)S(1)} %slice.12, f32[128,128]{1,0:T(8,128)S(1)} %copy-done.6), kind=kOutput, calls=%fused_computation.10 | convolution fusion | flops 67764224 | bytes 2359296 | tf_op jit(solution)/shard_map/bthe,bhde->bthd/dot_general | solution.py:86
  (35 shorter events, 0.2 us)
Async XLA Ops:
  0.6 5.2 %copy-start = (bf16[2048,128]{1,0:T(8,128)(2,1)S(1)}, bf16[2048,128]{1,0:T(8,128)(2,1)}, u32[]{:S(2)}) copy-start(bf16[2048,128]{1,0:T(8,128)(2,1)} %param.5) | copy-start | bytes 1572868
  2.3 5.5 %copy-start.2 = (bf16[2048,128]{1,0:T(8,128)(2,1)S(1)}, bf16[2048,128]{1,0:T(8,128)(2,1)}, u32[]{:S(2)}) copy-start(bf16[2048,128]{1,0:T(8,128)(2,1)} %param.7) | copy-start | bytes 1572868
  2.3 7.2 %collective-permute-start = (f32[1,1,128,128]{3,2,1,0:T(8,128)S(1)}, f32[1,1,128,128]{3,2,1,0:T(8,128)}, u32[]{:S(2)}, u32[]{:S(2)}) collective-permute-start(f32[1,1,128,128]{3,2,1,0:T(8,128)S(1)} %bitcast.99), channel_id=1, source_target_pairs={{0,4},{4,8},{8,12},{12,16},{16,20},{20,24},{24,28},{28,0},{1,5},{5... | collective-permute-start | bytes 196616 | tf_op jit(solution)/shard_map/ppermute | solution.py:29
  2.8 8.6 %collective-permute-start.1 = (f32[1,1,128,128]{3,2,1,0:T(8,128)S(1)}, f32[1,1,128,128]{3,2,1,0:T(8,128)S(1)}, u32[]{:S(2)}, u32[]{:S(2)}) collective-permute-start(f32[1,1,128,128]{3,2,1,0:T(8,128)S(1)} %bitcast.100), channel_id=1, source_target_pairs={{0,28},{4,0},{8,4},{12,8},{16,12},{20,16},{24,20},{28,24},{1,29},{... | collective-permute-start | bytes 196616 | tf_op jit(solution)/shard_map/ppermute | solution.py:34
  5.8 3.6 %copy-start.8 = (pred[512,512]{1,0:T(8,128)(4,1)}, pred[512,512]{1,0:T(8,128)(4,1)S(1)}, u32[]{:S(2)}) copy-start(pred[512,512]{1,0:T(8,128)(4,1)S(1)} %iota_compare_fusion) | copy-start | bytes 786436
  9.4 4.9 %collective-permute-start.2 = (f32[1,1,128,128]{3,2,1,0:T(8,128)}, f32[1,1,128,128]{3,2,1,0:T(8,128)}, u32[]{:S(2)}, u32[]{:S(2)}) collective-permute-start(f32[1,1,128,128]{3,2,1,0:T(8,128)} %collective-permute-done), channel_id=1, source_target_pairs={{0,4},{4,8},{8,12},{12,16},{16,20},{20,24},{24,28},{28,0},{1,5},{5... | collective-permute-start | bytes 196616 | tf_op jit(solution)/shard_map/ppermute | solution.py:29
  9.6 24.9 %copy-start.10 = (f32[128]{0:T(128)S(1)}, f32[128]{0:T(128)}, u32[]{:S(2)}) copy-start(f32[128]{0:T(128)} %param.8) | copy-start | bytes 1540
  11.4 4.9 %collective-permute-start.3 = (f32[1,1,128,128]{3,2,1,0:T(8,128)S(1)}, f32[1,1,128,128]{3,2,1,0:T(8,128)}, u32[]{:S(2)}, u32[]{:S(2)}) collective-permute-start(f32[1,1,128,128]{3,2,1,0:T(8,128)S(1)} %collective-permute-done.1), channel_id=1, source_target_pairs={{0,28},{4,0},{8,4},{12,8},{16,12},{20,16},{24,20},{28,24},{1,29},{... | collective-permute-start | bytes 196616 | tf_op jit(solution)/shard_map/ppermute | solution.py:34
  14.3 4.8 %collective-permute-start.4 = (f32[1,1,128,128]{3,2,1,0:T(8,128)}, f32[1,1,128,128]{3,2,1,0:T(8,128)S(1)}, u32[]{:S(2)}, u32[]{:S(2)}) collective-permute-start(f32[1,1,128,128]{3,2,1,0:T(8,128)} %collective-permute-done.2), channel_id=1, source_target_pairs={{0,4},{4,8},{8,12},{12,16},{16,20},{20,24},{24,28},{28,0},{1,5},{5... | collective-permute-start | bytes 196616 | tf_op jit(solution)/shard_map/ppermute | solution.py:29
  16.3 13.1 %collective-permute-start.5 = (f32[1,1,128,128]{3,2,1,0:T(8,128)}, f32[1,1,128,128]{3,2,1,0:T(8,128)}, u32[]{:S(2)}, u32[]{:S(2)}) collective-permute-start(f32[1,1,128,128]{3,2,1,0:T(8,128)} %collective-permute-done.3), channel_id=1, source_target_pairs={{0,28},{4,0},{8,4},{12,8},{16,12},{20,16},{24,20},{28,24},{1,29},{... | collective-permute-start | bytes 196616 | tf_op jit(solution)/shard_map/ppermute | solution.py:34
  19.2 12.6 %collective-permute-start.6 = (f32[1,1,128,128]{3,2,1,0:T(8,128)S(1)}, f32[1,1,128,128]{3,2,1,0:T(8,128)}, u32[]{:S(2)}, u32[]{:S(2)}) collective-permute-start(f32[1,1,128,128]{3,2,1,0:T(8,128)S(1)} %collective-permute-done.4), channel_id=1, source_target_pairs={{0,4},{4,8},{8,12},{12,16},{16,20},{20,24},{24,28},{28,0},{1,5},{5... | collective-permute-start | bytes 196616 | tf_op jit(solution)/shard_map/ppermute | solution.py:29
  34.5 22.5 %copy-start.5 = (f32[128,128]{1,0:T(8,128)}, f32[128,128]{1,0:T(8,128)S(1)}, u32[]{:S(2)}) copy-start(f32[128,128]{1,0:T(8,128)S(1)} %copy.47) | copy-start | bytes 196612
  59.8 2.6 %copy-start.3 = (bf16[2048,128]{1,0:T(8,128)(2,1)S(1)}, bf16[2048,128]{1,0:T(8,128)(2,1)}, u32[]{:S(2)}) copy-start(bf16[2048,128]{1,0:T(8,128)(2,1)} %param.7) | copy-start | bytes 1572868
  59.8 2.6 %copy-start.9 = (pred[512,512]{1,0:T(8,128)(4,1)S(1)}, pred[512,512]{1,0:T(8,128)(4,1)}, u32[]{:S(2)}) copy-start(pred[512,512]{1,0:T(8,128)(4,1)} %copy-done.8) | copy-start | bytes 786436
  63.2 1.9 %copy-start.1 = (bf16[2048,128]{1,0:T(8,128)(2,1)S(1)}, bf16[2048,128]{1,0:T(8,128)(2,1)}, u32[]{:S(2)}) copy-start(bf16[2048,128]{1,0:T(8,128)(2,1)} %param.6) | copy-start | bytes 1572868
  78.8 6.3 %copy-start.4 = (bf16[2048,128]{1,0:T(8,128)(2,1)S(1)}, bf16[2048,128]{1,0:T(8,128)(2,1)}, u32[]{:S(2)}) copy-start(bf16[2048,128]{1,0:T(8,128)(2,1)} %param.7) | copy-start | bytes 1572868
  80.1 0.6 copy-start.7
  83.1 4.4 %copy-start.6 = (f32[128,128]{1,0:T(8,128)S(1)}, f32[128,128]{1,0:T(8,128)}, u32[]{:S(2)}) copy-start(f32[128,128]{1,0:T(8,128)} %copy-done.5) | copy-start | bytes 196612
